TPU v7x, 32 devices: a whole 2x2x4 slice. The times are simulated.
32 devices in a mesh: section: 4 (over y, x), seq: 8 (over z, core).
Axes of the slice: x: 2, y: 2, z: 4, core: 2. Of those that a mesh axis runs over, the one named last changes fastest.
Arguments:
- queries: bfloat16 [4, 1024, 4096], P('section', 'seq'), may hold values from -120 to 120
- grad_out: bfloat16 [4, 1024, 4096], P('section', 'seq'), may hold values from -6 to 6
- keys: bfloat16 [1024, 1024], P('seq', 'section'), may hold values from -5.5 to 5.5
- values: bfloat16 [1024, 1024], P('seq', 'section'), may hold values from -6 to 6
- key_first: int32 [8], P('seq'), may hold values from 0 to 7, as said below
Outputs:
- grad_queries: bfloat16 [4, 1024, 4096], P('section', 'seq')
- grad_keys: float32 [1024, 1024], P('seq', 'section')
- grad_values: float32 [1024, 1024], P('seq', 'section')
Inputs may be any that keep to these rules, and one draw needn't show every extreme that they name: s - 1 <= key_first[s] <= s and key_first[s] >= 0; in every draw some shard s >= 1 has key_first[s] = s - 1.
All inputs are finite; a program needn't handle non-finite values.
Results may differ from a plain program's by a relative error of at most 0.008.
Values may be sent and summed in bfloat16 or wider, within the bound.
No kernel may reach another device: no remote copies, remote signals or barrier semaphores. Data moves between devices by JAX's collectives and lax.ppermute only.
A program may use at most 64 MiB of HBM per device.

v0:
```python
import functools
import math

import jax
import jax.numpy as jnp
from jax import lax
from jax.experimental import pallas as pl
from jax.experimental.pallas import tpu as pltpu
from jax.sharding import PartitionSpec as P

HEADS = 32
KV_HEADS = 8
HEAD_DIM = 128
GROUP = HEADS // KV_HEADS
MASKED = -1e30
SCALE = 1.0 / math.sqrt(HEAD_DIM)
EXP2_SCALE = SCALE * math.log2(math.e)

NT = (((1,), (1,)), ((), ()))
NN = (((1,), (0,)), ((), ()))
TN = (((0,), (0,)), ((), ()))


def exchanged(x, partner_of):
    sections, shards = lax.axis_size("section"), lax.axis_size("seq")
    pairs = []
    for i in range(sections):
        for s in range(shards):
            j, t = partner_of(i, s, shards)
            pairs.append((i * shards + s, j * shards + t))
    return lax.ppermute(x, ("section", "seq"), pairs)


def swap_section(x, flip):
    return exchanged(x, lambda i, s, shards: (i ^ flip, s))


def rotate_seq(x, by):
    return exchanged(x, lambda i, s, shards: (i, (s + by) % shards))


def dot(a, b, dims):
    return lax.dot_general(a, b, dims, preferred_element_type=jnp.float32)


def softmax_grads(scores, dprob, bias, causal):
    tok = causal.shape[0]
    dscores, wrounds = [], []
    for a in range(GROUP):
        head = slice(a * tok, (a + 1) * tok)
        parts = [jnp.where(causal, scores[-tok:, head], MASKED)]
        grads = [dprob[-tok:, head]]
        if bias is not None:
            parts.insert(0, scores[:tok, head] + bias)
            grads.insert(0, dprob[:tok, head])
        top = jnp.max(functools.reduce(jnp.maximum, parts), axis=0, keepdims=True)
        probs = [jnp.exp2((part - top) * EXP2_SCALE) for part in parts]
        inv = 1.0 / jnp.sum(sum(probs), axis=0, keepdims=True)
        mixed = sum(p * d for p, d in zip(probs, grads))
        row_dot = jnp.sum(mixed, axis=0, keepdims=True) * inv
        weights = [p * inv for p in probs]
        dscores.append([w * (d - row_dot) * SCALE for w, d in zip(weights, grads)])
        wrounds.append(weights)
    return [
        jnp.concatenate(
            [jnp.concatenate([x.astype(jnp.bfloat16) for x in parts], axis=0) for parts in heads],
            axis=1,
        )
        for heads in (dscores, wrounds)
    ]


def load_kernel(slices, first_ref, q_hbm, g_hbm, *refs):
    q_outs, g_outs = refs[:slices], refs[slices : 2 * slices]
    bias_out, sems = refs[2 * slices :]
    place = lax.axis_index("section")
    width = q_outs[0].shape[1]
    copies = []
    for flip in range(slices):
        span = pl.ds(pl.multiple_of((place ^ flip) * width, width), width)
        copies.append(pltpu.make_async_copy(q_hbm.at[:, span], q_outs[flip], sems.at[0, flip]))
        copies.append(pltpu.make_async_copy(g_hbm.at[:, span], g_outs[flip], sems.at[1, flip]))
    for copy in copies:
        copy.start()
    seen = first_ref[0] < lax.axis_index("seq")
    bias_out[...] = jnp.full(bias_out.shape, jnp.where(seen, 0.0, MASKED), jnp.float32)
    for copy in copies:
        copy.wait()


def store_kernel(slices, *refs):
    dq_ins, dq_hbm, sems = refs[:slices], refs[slices], refs[slices + 1]
    place = lax.axis_index("section")
    width = dq_ins[0].shape[1]
    copies = []
    for flip in range(slices):
        span = pl.ds(pl.multiple_of((place ^ flip) * width, width), width)
        copies.append(pltpu.make_async_copy(dq_ins[flip], dq_hbm.at[:, span], sems.at[flip]))
    for copy in copies:
        copy.start()
    for copy in copies:
        copy.wait()


def attention_kernel(bias_ref, q_ref, g_ref, own_ref, prev_ref, *refs):
    _, tok, width = own_ref.shape
    dq_out, own_out, prev_out = refs[-3:]
    for ref in refs[:-3]:
        ref[...] = bias_ref[...]
    key_pos = lax.broadcasted_iota(jnp.int32, (tok, tok), 0)
    query_pos = lax.broadcasted_iota(jnp.int32, (tok, tok), 1)
    causal = key_pos <= query_pos

    def work(bias):
        groups = []
        for h in range(width // HEAD_DIM):
            cols = slice(h * HEAD_DIM, (h + 1) * HEAD_DIM)
            heads = [
                slice((h * GROUP + a) * HEAD_DIM, (h * GROUP + a + 1) * HEAD_DIM)
                for a in range(GROUP)
            ]
            q4 = jnp.concatenate([q_ref[:, c] for c in heads], axis=0)
            g4 = jnp.concatenate([g_ref[:, c] for c in heads], axis=0)
            k2, v2 = own_ref[0, :, cols], own_ref[1, :, cols]
            if bias is not None:
                k2 = jnp.concatenate([prev_ref[0, :, cols], k2], axis=0)
                v2 = jnp.concatenate([prev_ref[1, :, cols], v2], axis=0)
            groups.append((cols, heads, q4, g4, k2, dot(k2, q4, NT), dot(v2, g4, NT)))
        rounded = [softmax_grads(scores, dprob, bias, causal) for *_, scores, dprob in groups]
        results = []
        for (_, _, q4, g4, k2, _, _), (dscore, wround) in zip(groups, rounded):
            dq_t = dot(k2, dscore, TN).astype(jnp.bfloat16)
            results.append((dq_t, dot(dscore, q4, NN), dot(wround, g4, NN)))
        for (cols, heads, *_), (dq_t, dk, dv) in zip(groups, results):
            for a, head in enumerate(heads):
                dq_out[:, head] = dq_t[:, a * tok : (a + 1) * tok].T
            for kind, grad in enumerate((dk, dv)):
                own_out[kind, :, cols] = grad[-tok:]
                if bias is not None:
                    prev_out[kind, :, cols] = grad[:tok].astype(jnp.bfloat16)

    @pl.when(lax.axis_index("seq") > 0)
    def _():
        work(bias_ref[0:1, 0:1])

    @pl.when(lax.axis_index("seq") == 0)
    def _():
        prev_out[...] = jnp.zeros(prev_out.shape, prev_out.dtype)
        work(None)


def after(x, token):
    return lax.optimization_barrier((x, token))[0]


def body(queries, grad_out, keys, values, key_first):
    slices = lax.axis_size("section")
    tok, width = keys.shape
    q_width = GROUP * width
    vmem = pl.BlockSpec(memory_space=pltpu.VMEM)
    hbm = pl.BlockSpec(memory_space=pltpu.HBM)
    params = pltpu.CompilerParams(vmem_limit_bytes=16 * 1024 * 1024)
    q_slice = jax.ShapeDtypeStruct((tok, q_width), jnp.bfloat16)
    tile = jax.ShapeDtypeStruct((8, 128), jnp.float32)
    order = [0] + list(range(slices - 1, 0, -1))

    pair = jnp.stack([keys, values])
    own = {flip: swap_section(pair, flip) for flip in order[1:]}
    own[0] = pair
    prev = {0: rotate_seq(pair, 1)}
    loaded = pl.pallas_call(
        functools.partial(load_kernel, slices),
        out_shape=[q_slice] * (2 * slices) + [tile],
        in_specs=[pl.BlockSpec(memory_space=pltpu.SMEM), hbm, hbm],
        out_specs=[vmem] * (2 * slices + 1),
        scratch_shapes=[pltpu.SemaphoreType.DMA((2, slices))],
        compiler_params=params,
        name="load_slices",
    )(
        key_first,
        pltpu.with_memory_space_constraint(queries[0], pltpu.HBM),
        pltpu.with_memory_space_constraint(grad_out[0], pltpu.HBM),
    )
    bias = loaded[-1]
    prev[order[1]] = rotate_seq(after(own[order[1]], bias), 1)
    bias = after(bias, own[order[1]])
    total, dq_parts, own_grads, back = None, {}, {}, {}
    for step, flip in enumerate(order):
        last = step == slices - 1
        *_, dq_parts[flip], own_grads[flip], held = out = pl.pallas_call(
            attention_kernel,
            out_shape=[tile] * (not last)
            + [
                q_slice,
                jax.ShapeDtypeStruct(pair.shape, jnp.float32),
                jax.ShapeDtypeStruct(pair.shape, jnp.bfloat16),
            ],
            in_specs=[vmem] * 5,
            out_specs=[vmem] * (3 if last else 4),
            compiler_params=params,
            name="attention_backward",
        )(bias, loaded[flip], loaded[slices + flip], own[flip], prev[flip])
        bias = out[0]
        if step == 0:
            back[0] = rotate_seq(held, -1)
            for later in order[2:]:
                prev[later] = rotate_seq(after(own[later], bias), 1)
            bias = after(bias, [own[later] for later in order])
        else:
            back[flip] = rotate_seq(held, -1)
    back[order[1]] = after(back[order[1]], back[0])
    for flip in order[1:]:
        part = own_grads[flip] + back[flip].astype(jnp.float32)
        part = part.astype(jnp.bfloat16)
        landed = swap_section(part, flip).astype(jnp.float32)
        total = landed if total is None else total + landed
    total = total + (own_grads[0] + back[0].astype(jnp.float32))
    dq = pl.pallas_call(
        functools.partial(store_kernel, slices),
        out_shape=jax.ShapeDtypeStruct(queries.shape[1:], jnp.bfloat16),
        in_specs=[vmem] * slices,
        out_specs=hbm,
        scratch_shapes=[pltpu.SemaphoreType.DMA((slices,))],
        compiler_params=params,
        name="store_slices",
    )(*[dq_parts[flip] for flip in range(slices)])
    return (dq[None], total[0], total[1])


def solution(mesh):
    placed = (
        P("section", "seq", None),
        P("section", "seq", None),
        P("seq", "section"),
        P("seq", "section"),
        P("seq"),
    )
    return jax.shard_map(
        body,
        mesh=mesh,
        in_specs=placed,
        out_specs=(P("section", "seq", None), P("seq", "section"), P("seq", "section")),
        check_vma=False,
    )
```

profile of v0, /device:TPU:0, one launch (start us, length us, event | category | flops | bytes accessed | tf_op | source)
XLA Modules:
  0.0 32.5 jit_solution(14838399572344932091)
XLA Ops:
  0.6 0.9 %pad_maximum_fusion.own_ref = bf16[2,128,256]{2,1,0:T(8,128)(2,1)S(1)} fusion(bf16[1,128,256]{2,1,0:T(8,128)(2,1)} %bitcast.12, bf16[1,128,256]{2,1,0:T(8,128)(2,1)} %bitcast.13), kind=kLoop, calls=%fused_computation.6 | loop fusion | flops 65536 | bytes 262144 | tf_op jit(solution)/shard_map/stack | solution.py:167
  1.5 4.0 %collective-permute-start = (bf16[2,128,256]{2,1,0:T(8,128)(2,1)S(1)}, bf16[2,128,256]{2,1,0:T(8,128)(2,1)S(1)}, u32[]{:S(2)}, u32[]{:S(2)}) collective-permute-start(bf16[2,128,256]{2,1,0:T(8,128)(2,1)S(1)} %pad_maximum_fusion.own_ref), channel_id=1, source_target_pairs={{0,24},{1,25},{2,26},{3,27},{4,28},{5,29},{6,30},{7,31},{8,16},{9,... | collective-permute-start | bytes 393224 | tf_op jit(solution)/shard_map/ppermute | solution.py:31
  5.5 0.0 collective-permute-start.1
  5.5 0.5 %collective-permute-start.2 = (bf16[2,128,256]{2,1,0:T(8,128)(2,1)S(1)}, bf16[2,128,256]{2,1,0:T(8,128)(2,1)S(1)}, u32[]{:S(2)}, u32[]{:S(2)}) collective-permute-start(bf16[2,128,256]{2,1,0:T(8,128)(2,1)S(1)} %pad_maximum_fusion.own_ref), channel_id=1, source_target_pairs={{0,16},{1,17},{2,18},{3,19},{4,20},{5,21},{6,22},{7,23},{8,24},{9,... | collective-permute-start | bytes 393224 | tf_op jit(solution)/shard_map/ppermute | solution.py:31
  6.0 0.2 collective-permute-start.3
  6.8 1.6 %load_slices.1 = (bf16[128,1024]{1,0:T(8,128)(2,1)S(1)}, bf16[128,1024]{1,0:T(8,128)(2,1)S(1)}, bf16[128,1024]{1,0:T(8,128)(2,1)S(1)}, bf16[128,1024]{1,0:T(8,12...) custom-call(s32[1]{0:T(128)S(6)} %copy.8.first_ref, ...), custom_call_target="tpu_custom_call" | custom-call | tf_op jit(solution)/shard_map/load_slices/pallas_call | solution.py:171
  8.4 0.5 %collective-permute-done.own_ref = bf16[2,128,256]{2,1,0:T(8,128)(2,1)S(1)} collective-permute-done((bf16[2,128,256]{2,1,0:T(8,128)(2,1)S(1)}, bf16[2,128,256]{2,1,0:T(8,128)(2,1)S(1)}, u32[]{:S(2)}, u32[]{:S(2)}) %collective-permute-start) | collective-permute-done | bytes 131104 | tf_op jit(solution)/shard_map/ppermute | solution.py:31
  9.0 1.0 %collective-permute-start.4 = (bf16[2,128,256]{2,1,0:T(8,128)(2,1)S(1)}, bf16[2,128,256]{2,1,0:T(8,128)(2,1)S(1)}, u32[]{:S(2)}, u32[]{:S(2)}) collective-permute-start(bf16[2,128,256]{2,1,0:T(8,128)(2,1)S(1)} %collective-permute-done.own_ref), channel_id=1, source_target_pairs={{0,1},{1,2},{2,3},{3,4},{4,5},{5,6},{6,7},{7,0},{8,9},{9,10},{10,1... | collective-permute-start | bytes 393224 | tf_op jit(solution)/shard_map/ppermute | solution.py:31
  10.0 1.7 %collective-permute-done.1.prev_ref = bf16[2,128,256]{2,1,0:T(8,128)(2,1)S(1)} collective-permute-done((bf16[2,128,256]{2,1,0:T(8,128)(2,1)S(1)}, bf16[2,128,256]{2,1,0:T(8,128)(2,1)S(1)}, u32[]{:S(2)}, u32[]{:S(2)}) %collective-permute-start.1) | collective-permute-done | bytes 131104 | tf_op jit(solution)/shard_map/ppermute | solution.py:31
  11.7 0.7 %attention_backward.4 = (f32[8,128]{1,0:T(8,128)S(1)}, bf16[128,1024]{1,0:T(8,128)(2,1)S(1)}, f32[2,128,256]{2,1,0:T(8,128)S(1)}, bf16[2,128,256]{2,1,0:T(8,128)(2,1)S(1)}) custom-call(f32[8,128]{1,0:T(8,128)S(1)} %get-tuple-element.34.bias_ref, bf16[128,1024]{1,0:T(8,128)(2,1)S(1)} %get-tuple-element.35.q_ref, ...), custom_call_target="tpu_custom_call" | custom-call | tf_op jit(solution)/shard_map/attention_backward/pallas_call | solution.py:190
  12.4 0.0 collective-permute-done.2.own_ref
  12.4 0.1 collective-permute-start.5
  12.5 0.0 collective-permute-done.3.own_ref
  12.5 0.6 %collective-permute-start.6 = (bf16[2,128,256]{2,1,0:T(8,128)(2,1)S(1)}, bf16[2,128,256]{2,1,0:T(8,128)(2,1)S(1)}, u32[]{:S(2)}, u32[]{:S(2)}) collective-permute-start(bf16[2,128,256]{2,1,0:T(8,128)(2,1)S(1)} %collective-permute-done.3.own_ref), channel_id=1, source_target_pairs={{0,1},{1,2},{2,3},{3,4},{4,5},{5,6},{6,7},{7,0},{8,9},{9,10},{10,1... | collective-permute-start | bytes 393224 | tf_op jit(solution)/shard_map/ppermute | solution.py:31
  13.1 3.0 %collective-permute-start.8 = (bf16[2,128,256]{2,1,0:T(8,128)(2,1)S(1)}, bf16[2,128,256]{2,1,0:T(8,128)(2,1)S(1)}, u32[]{:S(2)}, u32[]{:S(2)}) collective-permute-start(bf16[2,128,256]{2,1,0:T(8,128)(2,1)S(1)} %get-tuple-element.56), channel_id=1, source_target_pairs={{0,7},{1,0},{2,1},{3,2},{4,3},{5,4},{6,5},{7,6},{8,15},{9,8},{10,9... | collective-permute-start | bytes 393224 | tf_op jit(solution)/shard_map/ppermute | solution.py:31
  16.1 0.0 collective-permute-done.4.prev_ref
  16.1 0.7 %attention_backward.5 = (f32[8,128]{1,0:T(8,128)S(1)}, bf16[128,1024]{1,0:T(8,128)(2,1)S(1)}, f32[2,128,256]{2,1,0:T(8,128)S(1)}, bf16[2,128,256]{2,1,0:T(8,128)(2,1)S(1)}) custom-call(f32[8,128]{1,0:T(8,128)S(1)} %get-tuple-element.39.bias_ref, bf16[128,1024]{1,0:T(8,128)(2,1)S(1)} %get-tuple-element.40.q_ref, ...), custom_call_target="tpu_custom_call" | custom-call | tf_op jit(solution)/shard_map/attention_backward/pallas_call | solution.py:190
  16.8 1.0 %collective-permute-start.7 = (bf16[2,128,256]{2,1,0:T(8,128)(2,1)S(1)}, bf16[2,128,256]{2,1,0:T(8,128)(2,1)S(1)}, u32[]{:S(2)}, u32[]{:S(2)}) collective-permute-start(bf16[2,128,256]{2,1,0:T(8,128)(2,1)S(1)} %get-tuple-element.55), channel_id=1, source_target_pairs={{0,7},{1,0},{2,1},{3,2},{4,3},{5,4},{6,5},{7,6},{8,15},{9,8},{10,9... | collective-permute-start | bytes 393224 | tf_op jit(solution)/shard_map/ppermute | solution.py:31
  17.8 1.0 %collective-permute-done.5.prev_ref = bf16[2,128,256]{2,1,0:T(8,128)(2,1)S(1)} collective-permute-done((bf16[2,128,256]{2,1,0:T(8,128)(2,1)S(1)}, bf16[2,128,256]{2,1,0:T(8,128)(2,1)S(1)}, u32[]{:S(2)}, u32[]{:S(2)}) %collective-permute-start.5) | collective-permute-done | bytes 131104 | tf_op jit(solution)/shard_map/ppermute | solution.py:31
  18.8 0.7 %attention_backward.6 = (f32[8,128]{1,0:T(8,128)S(1)}, bf16[128,1024]{1,0:T(8,128)(2,1)S(1)}, f32[2,128,256]{2,1,0:T(8,128)S(1)}, bf16[2,128,256]{2,1,0:T(8,128)(2,1)S(1)}) custom-call(f32[8,128]{1,0:T(8,128)S(1)} %get-tuple-element.43.bias_ref, bf16[128,1024]{1,0:T(8,128)(2,1)S(1)} %get-tuple-element.44.q_ref, ...), custom_call_target="tpu_custom_call" | custom-call | tf_op jit(solution)/shard_map/attention_backward/pallas_call | solution.py:190
  19.6 0.5 %collective-permute-start.10 = (bf16[2,128,256]{2,1,0:T(8,128)(2,1)S(1)}, bf16[2,128,256]{2,1,0:T(8,128)(2,1)S(1)}, u32[]{:S(2)}, u32[]{:S(2)}) collective-permute-start(bf16[2,128,256]{2,1,0:T(8,128)(2,1)S(1)} %get-tuple-element.59), channel_id=1, source_target_pairs={{0,7},{1,0},{2,1},{3,2},{4,3},{5,4},{6,5},{7,6},{8,15},{9,8},{10,9... | collective-permute-start | bytes 393224 | tf_op jit(solution)/shard_map/ppermute | solution.py:31
  20.1 1.1 %collective-permute-done.6.prev_ref = bf16[2,128,256]{2,1,0:T(8,128)(2,1)S(1)} collective-permute-done((bf16[2,128,256]{2,1,0:T(8,128)(2,1)S(1)}, bf16[2,128,256]{2,1,0:T(8,128)(2,1)S(1)}, u32[]{:S(2)}, u32[]{:S(2)}) %collective-permute-start.6) | collective-permute-done | bytes 131104 | tf_op jit(solution)/shard_map/ppermute | solution.py:31
  21.1 0.7 %attention_backward.7 = (bf16[128,1024]{1,0:T(8,128)(2,1)S(1)}, f32[2,128,256]{2,1,0:T(8,128)S(1)}, bf16[2,128,256]{2,1,0:T(8,128)(2,1)S(1)}) custom-call(f32[8,128]{1,0:T(8,128)S(1)} %get-tuple-element.47.bias_ref, bf16[128,1024]{1,0:T(8,128)(2,1)S(1)} %get-tuple-element.48.q_ref, bf16[128,1024]{1,0:T(8,128)(2,1)S(1)} %get-tuple-element.49.g_ref, ...), custom_call_target="tpu_custom_call" | custom-call | tf_op jit(solution)/shard_map/attention_backward/pallas_call | solution.py:190
  21.8 0.8 %collective-permute-start.12 = (bf16[2,128,256]{2,1,0:T(8,128)(2,1)S(1)}, bf16[2,128,256]{2,1,0:T(8,128)(2,1)S(1)}, u32[]{:S(2)}, u32[]{:S(2)}) collective-permute-start(bf16[2,128,256]{2,1,0:T(8,128)(2,1)S(1)} %get-tuple-element.61), channel_id=1, source_target_pairs={{0,7},{1,0},{2,1},{3,2},{4,3},{5,4},{6,5},{7,6},{8,15},{9,8},{10,9... | collective-permute-start | bytes 393224 | tf_op jit(solution)/shard_map/ppermute | solution.py:31
  22.6 0.0 collective-permute-done.8
  22.6 0.0 collective-permute-done.7
  22.7 2.4 %collective-permute-start.9 = (bf16[2,128,256]{2,1,0:T(8,128)(2,1)S(1)}, bf16[2,128,256]{2,1,0:T(8,128)(2,1)S(1)}, u32[]{:S(2)}, u32[]{:S(2)}) collective-permute-start(bf16[2,128,256]{2,1,0:T(8,128)(2,1)S(1)} %add_convert_fusion.2), channel_id=1, source_target_pairs={{0,24},{1,25},{2,26},{3,27},{4,28},{5,29},{6,30},{7,31},{8,16},{9,... | collective-permute-start | bytes 393224 | tf_op jit(solution)/shard_map/ppermute | solution.py:31
  25.0 0.0 collective-permute-done.10
  25.1 0.7 %collective-permute-start.11 = (bf16[2,128,256]{2,1,0:T(8,128)(2,1)S(1)}, bf16[2,128,256]{2,1,0:T(8,128)(2,1)S(1)}, u32[]{:S(2)}, u32[]{:S(2)}) collective-permute-start(bf16[2,128,256]{2,1,0:T(8,128)(2,1)S(1)} %add_convert_fusion.1), channel_id=1, source_target_pairs={{0,16},{1,17},{2,18},{3,19},{4,20},{5,21},{6,22},{7,23},{8,24},{9,... | collective-permute-start | bytes 393224 | tf_op jit(solution)/shard_map/ppermute | solution.py:31
  25.8 0.0 collective-permute-done.12
  25.8 0.9 %collective-permute-start.13 = (bf16[2,128,256]{2,1,0:T(8,128)(2,1)S(1)}, bf16[2,128,256]{2,1,0:T(8,128)(2,1)S(1)}, u32[]{:S(2)}, u32[]{:S(2)}) collective-permute-start(bf16[2,128,256]{2,1,0:T(8,128)(2,1)S(1)} %add_convert_fusion), channel_id=1, source_target_pairs={{0,8},{1,9},{2,10},{3,11},{4,12},{5,13},{6,14},{7,15},{8,0},{9,1},... | collective-permute-start | bytes 393224 | tf_op jit(solution)/shard_map/ppermute | solution.py:31
  26.7 1.0 %store_slices.1 = bf16[128,4096]{1,0:T(8,128)(2,1)} custom-call(bf16[128,1024]{1,0:T(8,128)(2,1)S(1)} %get-tuple-element.37.refs_0_, bf16[128,1024]{1,0:T(8,128)(2,1)S(1)} %get-tuple-element.51.refs_1_, bf16[128,1024]{1,0:T(8,128)(2,1)S(1)} %get-tuple-element.52.refs_2_, bf16[128,1024]{1,0:T(8,128)(2,1)S(1)} %get-tuple-element.53.refs_3_), custom_call_target="tpu_custom_call" | custom-call | tf_op jit(solution)/shard_map/store_slices/pallas_call | solution.py:218
  27.7 1.2 %collective-permute-done.9 = bf16[2,128,256]{2,1,0:T(8,128)(2,1)S(1)} collective-permute-done((bf16[2,128,256]{2,1,0:T(8,128)(2,1)S(1)}, bf16[2,128,256]{2,1,0:T(8,128)(2,1)S(1)}, u32[]{:S(2)}, u32[]{:S(2)}) %collective-permute-start.9) | collective-permute-done | bytes 131104 | tf_op jit(solution)/shard_map/ppermute | solution.py:31
  29.0 2.7 %collective-permute-done.11 = bf16[2,128,256]{2,1,0:T(8,128)(2,1)S(1)} collective-permute-done((bf16[2,128,256]{2,1,0:T(8,128)(2,1)S(1)}, bf16[2,128,256]{2,1,0:T(8,128)(2,1)S(1)}, u32[]{:S(2)}, u32[]{:S(2)}) %collective-permute-start.11) | collective-permute-done | bytes 131104 | tf_op jit(solution)/shard_map/ppermute | solution.py:31
  31.7 0.0 collective-permute-done.13
  31.7 0.1 add_add_fusion
  31.8 0.7 %slice_bitcast_fusion = (f32[128,256]{1,0:T(8,128)}, f32[128,256]{1,0:T(8,128)}) fusion(f32[2,128,256]{2,1,0:T(8,128)S(1)} %add_add_fusion), kind=kLoop, calls=%fused_computation.4 | loop fusion | bytes 524288 | tf_op jit(solution)/shard_map/squeeze | solution.py:227
  (3 shorter events, 0.1 us)
Async XLA Ops:
  1.5 7.5 %collective-permute-start = (bf16[2,128,256]{2,1,0:T(8,128)(2,1)S(1)}, bf16[2,128,256]{2,1,0:T(8,128)(2,1)S(1)}, u32[]{:S(2)}, u32[]{:S(2)}) collective-permute-start(bf16[2,128,256]{2,1,0:T(8,128)(2,1)S(1)} %pad_maximum_fusion.own_ref), channel_id=1, source_target_pairs={{0,24},{1,25},{2,26},{3,27},{4,28},{5,29},{6,30},{7,31},{8,16},{9,... | collective-permute-start | bytes 393224 | tf_op jit(solution)/shard_map/ppermute | solution.py:31
  5.5 6.2 %collective-permute-start.1 = (bf16[2,128,256]{2,1,0:T(8,128)(2,1)S(1)}, bf16[2,128,256]{2,1,0:T(8,128)(2,1)S(1)}, u32[]{:S(2)}, u32[]{:S(2)}) collective-permute-start(bf16[2,128,256]{2,1,0:T(8,128)(2,1)S(1)} %pad_maximum_fusion.own_ref), channel_id=1, source_target_pairs={{0,1},{1,2},{2,3},{3,4},{4,5},{5,6},{6,7},{7,0},{8,9},{9,10},{10,1... | collective-permute-start | bytes 393224 | tf_op jit(solution)/shard_map/ppermute | solution.py:31
  5.5 6.9 %collective-permute-start.2 = (bf16[2,128,256]{2,1,0:T(8,128)(2,1)S(1)}, bf16[2,128,256]{2,1,0:T(8,128)(2,1)S(1)}, u32[]{:S(2)}, u32[]{:S(2)}) collective-permute-start(bf16[2,128,256]{2,1,0:T(8,128)(2,1)S(1)} %pad_maximum_fusion.own_ref), channel_id=1, source_target_pairs={{0,16},{1,17},{2,18},{3,19},{4,20},{5,21},{6,22},{7,23},{8,24},{9,... | collective-permute-start | bytes 393224 | tf_op jit(solution)/shard_map/ppermute | solution.py:31
  6.0 6.5 %collective-permute-start.3 = (bf16[2,128,256]{2,1,0:T(8,128)(2,1)S(1)}, bf16[2,128,256]{2,1,0:T(8,128)(2,1)S(1)}, u32[]{:S(2)}, u32[]{:S(2)}) collective-permute-start(bf16[2,128,256]{2,1,0:T(8,128)(2,1)S(1)} %pad_maximum_fusion.own_ref), channel_id=1, source_target_pairs={{0,8},{1,9},{2,10},{3,11},{4,12},{5,13},{6,14},{7,15},{8,0},{9,1},... | collective-permute-start | bytes 393224 | tf_op jit(solution)/shard_map/ppermute | solution.py:31
  9.0 7.1 %collective-permute-start.4 = (bf16[2,128,256]{2,1,0:T(8,128)(2,1)S(1)}, bf16[2,128,256]{2,1,0:T(8,128)(2,1)S(1)}, u32[]{:S(2)}, u32[]{:S(2)}) collective-permute-start(bf16[2,128,256]{2,1,0:T(8,128)(2,1)S(1)} %collective-permute-done.own_ref), channel_id=1, source_target_pairs={{0,1},{1,2},{2,3},{3,4},{4,5},{5,6},{6,7},{7,0},{8,9},{9,10},{10,1... | collective-permute-start | bytes 393224 | tf_op jit(solution)/shard_map/ppermute | solution.py:31
  12.4 6.4 %collective-permute-start.5 = (bf16[2,128,256]{2,1,0:T(8,128)(2,1)S(1)}, bf16[2,128,256]{2,1,0:T(8,128)(2,1)S(1)}, u32[]{:S(2)}, u32[]{:S(2)}) collective-permute-start(bf16[2,128,256]{2,1,0:T(8,128)(2,1)S(1)} %collective-permute-done.2.own_ref), channel_id=1, source_target_pairs={{0,1},{1,2},{2,3},{3,4},{4,5},{5,6},{6,7},{7,0},{8,9},{9,10},{10,1... | collective-permute-start | bytes 393224 | tf_op jit(solution)/shard_map/ppermute | solution.py:31
  12.5 8.6 %collective-permute-start.6 = (bf16[2,128,256]{2,1,0:T(8,128)(2,1)S(1)}, bf16[2,128,256]{2,1,0:T(8,128)(2,1)S(1)}, u32[]{:S(2)}, u32[]{:S(2)}) collective-permute-start(bf16[2,128,256]{2,1,0:T(8,128)(2,1)S(1)} %collective-permute-done.3.own_ref), channel_id=1, source_target_pairs={{0,1},{1,2},{2,3},{3,4},{4,5},{5,6},{6,7},{7,0},{8,9},{9,10},{10,1... | collective-permute-start | bytes 393224 | tf_op jit(solution)/shard_map/ppermute | solution.py:31
  13.1 9.5 %collective-permute-start.8 = (bf16[2,128,256]{2,1,0:T(8,128)(2,1)S(1)}, bf16[2,128,256]{2,1,0:T(8,128)(2,1)S(1)}, u32[]{:S(2)}, u32[]{:S(2)}) collective-permute-start(bf16[2,128,256]{2,1,0:T(8,128)(2,1)S(1)} %get-tuple-element.56), channel_id=1, source_target_pairs={{0,7},{1,0},{2,1},{3,2},{4,3},{5,4},{6,5},{7,6},{8,15},{9,8},{10,9... | collective-permute-start | bytes 393224 | tf_op jit(solution)/shard_map/ppermute | solution.py:31
  16.8 5.8 %collective-permute-start.7 = (bf16[2,128,256]{2,1,0:T(8,128)(2,1)S(1)}, bf16[2,128,256]{2,1,0:T(8,128)(2,1)S(1)}, u32[]{:S(2)}, u32[]{:S(2)}) collective-permute-start(bf16[2,128,256]{2,1,0:T(8,128)(2,1)S(1)} %get-tuple-element.55), channel_id=1, source_target_pairs={{0,7},{1,0},{2,1},{3,2},{4,3},{5,4},{6,5},{7,6},{8,15},{9,8},{10,9... | collective-permute-start | bytes 393224 | tf_op jit(solution)/shard_map/ppermute | solution.py:31
  19.6 5.5 %collective-permute-start.10 = (bf16[2,128,256]{2,1,0:T(8,128)(2,1)S(1)}, bf16[2,128,256]{2,1,0:T(8,128)(2,1)S(1)}, u32[]{:S(2)}, u32[]{:S(2)}) collective-permute-start(bf16[2,128,256]{2,1,0:T(8,128)(2,1)S(1)} %get-tuple-element.59), channel_id=1, source_target_pairs={{0,7},{1,0},{2,1},{3,2},{4,3},{5,4},{6,5},{7,6},{8,15},{9,8},{10,9... | collective-permute-start | bytes 393224 | tf_op jit(solution)/shard_map/ppermute | solution.py:31
  21.8 4.0 %collective-permute-start.12 = (bf16[2,128,256]{2,1,0:T(8,128)(2,1)S(1)}, bf16[2,128,256]{2,1,0:T(8,128)(2,1)S(1)}, u32[]{:S(2)}, u32[]{:S(2)}) collective-permute-start(bf16[2,128,256]{2,1,0:T(8,128)(2,1)S(1)} %get-tuple-element.61), channel_id=1, source_target_pairs={{0,7},{1,0},{2,1},{3,2},{4,3},{5,4},{6,5},{7,6},{8,15},{9,8},{10,9... | collective-permute-start | bytes 393224 | tf_op jit(solution)/shard_map/ppermute | solution.py:31
  22.7 6.3 %collective-permute-start.9 = (bf16[2,128,256]{2,1,0:T(8,128)(2,1)S(1)}, bf16[2,128,256]{2,1,0:T(8,128)(2,1)S(1)}, u32[]{:S(2)}, u32[]{:S(2)}) collective-permute-start(bf16[2,128,256]{2,1,0:T(8,128)(2,1)S(1)} %add_convert_fusion.2), channel_id=1, source_target_pairs={{0,24},{1,25},{2,26},{3,27},{4,28},{5,29},{6,30},{7,31},{8,16},{9,... | collective-permute-start | bytes 393224 | tf_op jit(solution)/shard_map/ppermute | solution.py:31
  25.1 6.6 %collective-permute-start.11 = (bf16[2,128,256]{2,1,0:T(8,128)(2,1)S(1)}, bf16[2,128,256]{2,1,0:T(8,128)(2,1)S(1)}, u32[]{:S(2)}, u32[]{:S(2)}) collective-permute-start(bf16[2,128,256]{2,1,0:T(8,128)(2,1)S(1)} %add_convert_fusion.1), channel_id=1, source_target_pairs={{0,16},{1,17},{2,18},{3,19},{4,20},{5,21},{6,22},{7,23},{8,24},{9,... | collective-permute-start | bytes 393224 | tf_op jit(solution)/shard_map/ppermute | solution.py:31
  25.8 5.8 %collective-permute-start.13 = (bf16[2,128,256]{2,1,0:T(8,128)(2,1)S(1)}, bf16[2,128,256]{2,1,0:T(8,128)(2,1)S(1)}, u32[]{:S(2)}, u32[]{:S(2)}) collective-permute-start(bf16[2,128,256]{2,1,0:T(8,128)(2,1)S(1)} %add_convert_fusion), channel_id=1, source_target_pairs={{0,8},{1,9},{2,10},{3,11},{4,12},{5,13},{6,14},{7,15},{8,0},{9,1},... | collective-permute-start | bytes 393224 | tf_op jit(solution)/shard_map/ppermute | solution.py:31
where the time goes:
time: 32.7 us; the launch traced here: 32.5 us
  starting transfers between devices  15.6 us (48%)
  waiting for transfers between devices  8.28 us (25%)
  Pallas kernels  5.43 us (17%)
  between operations  1.39 us (4%)
  other arithmetic  1.05 us (3%)
  local copies, waits for them, and re-layouts  0.72 us (2%)
    ppermute x14, starting transfers between devices, exchanged(): return lax.ppermute(x, ('section', 'seq'), pairs)  15.6 us
    ppermute x14, waiting for transfers between devices, exchanged(): return lax.ppermute(x, ('section', 'seq'), pairs)  8.28 us
    pallas_call x4, Pallas kernels, body(): pl.pallas_call(attention_kernel, out_shape=[tile] * (not last) + [q_slice...  2.85 us
    pallas_call x1, Pallas kernels, body(): pl.pallas_call(functools.partial(load_kernel, slices), out_shape=[q_slice...  1.59 us
    pallas_call x1, Pallas kernels, body(): pl.pallas_call(functools.partial(store_kernel, slices), out_shape=jax.Sha...  0.99 us
    another operation x1, other arithmetic, body(): pair = jnp.stack([keys, values])  0.89 us
    squeeze x1, local copies, waits for them, and re-layouts, body(): return (dq[None], total[0], total[1])  0.72 us
  transfers between devices with their start and end apart: 14, of which 6 were waited for; matrix products, arithmetic and copies ran while one was open for 0% of the time, Pallas kernels for 17%

commit v1 on v0

--- a/solution.py
+++ b/solution.py
@@ -202,12 +202,14 @@
         )(bias, loaded[flip], loaded[slices + flip], own[flip], prev[flip])
         bias = out[0]
         if step == 0:
-            back[0] = rotate_seq(held, -1)
+            first_held = held
             for later in order[2:]:
                 prev[later] = rotate_seq(after(own[later], bias), 1)
             bias = after(bias, [own[later] for later in order])
         else:
             back[flip] = rotate_seq(held, -1)
+        if step == 1:
+            back[0] = rotate_seq(after(first_held, bias), -1)
     back[order[1]] = after(back[order[1]], back[0])
     for flip in order[1:]:
         part = own_grads[flip] + back[flip].astype(jnp.float32)

time: 32.7 us -> 32.9 us (level)
  starting transfers between devices: 15.6 us -> 16.3 us
  waiting for transfers between devices: 8.28 us -> 7.84 us
    ppermute x14, starting transfers between devices: 15.6 us -> 16.3 us  [exchanged(): return lax.ppermute(x, ('section', 'seq'), pairs)]
    ppermute x14, waiting for transfers between devices: 8.28 us -> 7.84 us  [exchanged(): return lax.ppermute(x, ('section', 'seq'), pairs)]
where the time goes in v1:
time: 32.9 us; the launch traced here: 32.7 us
  starting transfers between devices  16.3 us (50%)
  waiting for transfers between devices  7.84 us (24%)
  Pallas kernels  5.43 us (17%)
  between operations  1.39 us (4%)
  other arithmetic  1.05 us (3%)
  local copies, waits for them, and re-layouts  0.72 us (2%)
    ppermute x14, starting transfers between devices, exchanged(): return lax.ppermute(x, ('section', 'seq'), pairs)  16.3 us
    ppermute x14, waiting for transfers between devices, exchanged(): return lax.ppermute(x, ('section', 'seq'), pairs)  7.84 us
    pallas_call x4, Pallas kernels, body(): pl.pallas_call(attention_kernel, out_shape=[tile] * (not last) + [q_slice...  2.85 us
    pallas_call x1, Pallas kernels, body(): pl.pallas_call(functools.partial(load_kernel, slices), out_shape=[q_slice...  1.59 us
    pallas_call x1, Pallas kernels, body(): pl.pallas_call(functools.partial(store_kernel, slices), out_shape=jax.Sha...  0.99 us
    another operation x1, other arithmetic, body(): pair = jnp.stack([keys, values])  0.89 us
    squeeze x1, local copies, waits for them, and re-layouts, body(): return (dq[None], total[0], total[1])  0.72 us
  transfers between devices with their start and end apart: 14, of which 6 were waited for; matrix products, arithmetic and copies ran while one was open for 0% of the time, Pallas kernels for 17%

profile of v1, /device:TPU:0, one launch (start us, length us, event | category | flops | bytes accessed | tf_op | source)
XLA Modules:
  0.0 32.7 jit_solution(8012463568875291634)
XLA Ops:
  0.6 0.9 %pad_maximum_fusion.own_ref = bf16[2,128,256]{2,1,0:T(8,128)(2,1)S(1)} fusion(bf16[1,128,256]{2,1,0:T(8,128)(2,1)} %bitcast.12, bf16[1,128,256]{2,1,0:T(8,128)(2,1)} %bitcast.13), kind=kLoop, calls=%fused_computation.6 | loop fusion | flops 65536 | bytes 262144 | tf_op jit(solution)/shard_map/stack | solution.py:167
  1.5 4.0 %collective-permute-start = (bf16[2,128,256]{2,1,0:T(8,128)(2,1)S(1)}, bf16[2,128,256]{2,1,0:T(8,128)(2,1)S(1)}, u32[]{:S(2)}, u32[]{:S(2)}) collective-permute-start(bf16[2,128,256]{2,1,0:T(8,128)(2,1)S(1)} %pad_maximum_fusion.own_ref), channel_id=1, source_target_pairs={{0,24},{1,25},{2,26},{3,27},{4,28},{5,29},{6,30},{7,31},{8,16},{9,... | collective-permute-start | bytes 393224 | tf_op jit(solution)/shard_map/ppermute | solution.py:31
  5.5 0.0 collective-permute-start.1
  5.5 0.5 %collective-permute-start.2 = (bf16[2,128,256]{2,1,0:T(8,128)(2,1)S(1)}, bf16[2,128,256]{2,1,0:T(8,128)(2,1)S(1)}, u32[]{:S(2)}, u32[]{:S(2)}) collective-permute-start(bf16[2,128,256]{2,1,0:T(8,128)(2,1)S(1)} %pad_maximum_fusion.own_ref), channel_id=1, source_target_pairs={{0,16},{1,17},{2,18},{3,19},{4,20},{5,21},{6,22},{7,23},{8,24},{9,... | collective-permute-start | bytes 393224 | tf_op jit(solution)/shard_map/ppermute | solution.py:31
  6.0 0.2 collective-permute-start.3
  6.8 1.6 %load_slices.1 = (bf16[128,1024]{1,0:T(8,128)(2,1)S(1)}, bf16[128,1024]{1,0:T(8,128)(2,1)S(1)}, bf16[128,1024]{1,0:T(8,128)(2,1)S(1)}, bf16[128,1024]{1,0:T(8,12...) custom-call(s32[1]{0:T(128)S(6)} %copy.8.first_ref, ...), custom_call_target="tpu_custom_call" | custom-call | tf_op jit(solution)/shard_map/load_slices/pallas_call | solution.py:171
  8.4 0.5 %collective-permute-done.own_ref = bf16[2,128,256]{2,1,0:T(8,128)(2,1)S(1)} collective-permute-done((bf16[2,128,256]{2,1,0:T(8,128)(2,1)S(1)}, bf16[2,128,256]{2,1,0:T(8,128)(2,1)S(1)}, u32[]{:S(2)}, u32[]{:S(2)}) %collective-permute-start) | collective-permute-done | bytes 131104 | tf_op jit(solution)/shard_map/ppermute | solution.py:31
  9.0 1.0 %collective-permute-start.4 = (bf16[2,128,256]{2,1,0:T(8,128)(2,1)S(1)}, bf16[2,128,256]{2,1,0:T(8,128)(2,1)S(1)}, u32[]{:S(2)}, u32[]{:S(2)}) collective-permute-start(bf16[2,128,256]{2,1,0:T(8,128)(2,1)S(1)} %collective-permute-done.own_ref), channel_id=1, source_target_pairs={{0,1},{1,2},{2,3},{3,4},{4,5},{5,6},{6,7},{7,0},{8,9},{9,10},{10,1... | collective-permute-start | bytes 393224 | tf_op jit(solution)/shard_map/ppermute | solution.py:31
  10.0 1.7 %collective-permute-done.1.prev_ref = bf16[2,128,256]{2,1,0:T(8,128)(2,1)S(1)} collective-permute-done((bf16[2,128,256]{2,1,0:T(8,128)(2,1)S(1)}, bf16[2,128,256]{2,1,0:T(8,128)(2,1)S(1)}, u32[]{:S(2)}, u32[]{:S(2)}) %collective-permute-start.1) | collective-permute-done | bytes 131104 | tf_op jit(solution)/shard_map/ppermute | solution.py:31
  11.7 0.7 %attention_backward.4 = (f32[8,128]{1,0:T(8,128)S(1)}, bf16[128,1024]{1,0:T(8,128)(2,1)S(1)}, f32[2,128,256]{2,1,0:T(8,128)S(1)}, bf16[2,128,256]{2,1,0:T(8,128)(2,1)S(1)}) custom-call(f32[8,128]{1,0:T(8,128)S(1)} %get-tuple-element.35.bias_ref, bf16[128,1024]{1,0:T(8,128)(2,1)S(1)} %get-tuple-element.36.q_ref, ...), custom_call_target="tpu_custom_call" | custom-call | tf_op jit(solution)/shard_map/attention_backward/pallas_call | solution.py:190
  12.4 0.0 collective-permute-done.2.own_ref
  12.4 0.0 collective-permute-done.3.own_ref
  12.4 0.1 collective-permute-start.5
  12.5 1.2 %collective-permute-start.6 = (bf16[2,128,256]{2,1,0:T(8,128)(2,1)S(1)}, bf16[2,128,256]{2,1,0:T(8,128)(2,1)S(1)}, u32[]{:S(2)}, u32[]{:S(2)}) collective-permute-start(bf16[2,128,256]{2,1,0:T(8,128)(2,1)S(1)} %collective-permute-done.3.own_ref), channel_id=1, source_target_pairs={{0,1},{1,2},{2,3},{3,4},{4,5},{5,6},{6,7},{7,0},{8,9},{9,10},{10,1... | collective-permute-start | bytes 393224 | tf_op jit(solution)/shard_map/ppermute | solution.py:31
  13.7 1.5 %collective-permute-done.4.prev_ref = bf16[2,128,256]{2,1,0:T(8,128)(2,1)S(1)} collective-permute-done((bf16[2,128,256]{2,1,0:T(8,128)(2,1)S(1)}, bf16[2,128,256]{2,1,0:T(8,128)(2,1)S(1)}, u32[]{:S(2)}, u32[]{:S(2)}) %collective-permute-start.4) | collective-permute-done | bytes 131104 | tf_op jit(solution)/shard_map/ppermute | solution.py:31
  15.2 0.7 %attention_backward.5 = (f32[8,128]{1,0:T(8,128)S(1)}, bf16[128,1024]{1,0:T(8,128)(2,1)S(1)}, f32[2,128,256]{2,1,0:T(8,128)S(1)}, bf16[2,128,256]{2,1,0:T(8,128)(2,1)S(1)}) custom-call(f32[8,128]{1,0:T(8,128)S(1)} %get-tuple-element.40.bias_ref, bf16[128,1024]{1,0:T(8,128)(2,1)S(1)} %get-tuple-element.41.q_ref, ...), custom_call_target="tpu_custom_call" | custom-call | tf_op jit(solution)/shard_map/attention_backward/pallas_call | solution.py:190
  15.9 1.5 %collective-permute-start.8 = (bf16[2,128,256]{2,1,0:T(8,128)(2,1)S(1)}, bf16[2,128,256]{2,1,0:T(8,128)(2,1)S(1)}, u32[]{:S(2)}, u32[]{:S(2)}) collective-permute-start(bf16[2,128,256]{2,1,0:T(8,128)(2,1)S(1)} %get-tuple-element.58), channel_id=1, source_target_pairs={{0,7},{1,0},{2,1},{3,2},{4,3},{5,4},{6,5},{7,6},{8,15},{9,8},{10,9... | collective-permute-start | bytes 393224 | tf_op jit(solution)/shard_map/ppermute | solution.py:31
  17.4 1.4 %collective-permute-start.7 = (bf16[2,128,256]{2,1,0:T(8,128)(2,1)S(1)}, bf16[2,128,256]{2,1,0:T(8,128)(2,1)S(1)}, u32[]{:S(2)}, u32[]{:S(2)}) collective-permute-start(bf16[2,128,256]{2,1,0:T(8,128)(2,1)S(1)} %get-tuple-element.56), channel_id=1, source_target_pairs={{0,7},{1,0},{2,1},{3,2},{4,3},{5,4},{6,5},{7,6},{8,15},{9,8},{10,9... | collective-permute-start | bytes 393224 | tf_op jit(solution)/shard_map/ppermute | solution.py:31
  18.8 0.0 collective-permute-done.5.prev_ref
  18.8 0.7 %attention_backward.6 = (f32[8,128]{1,0:T(8,128)S(1)}, bf16[128,1024]{1,0:T(8,128)(2,1)S(1)}, f32[2,128,256]{2,1,0:T(8,128)S(1)}, bf16[2,128,256]{2,1,0:T(8,128)(2,1)S(1)}) custom-call(f32[8,128]{1,0:T(8,128)S(1)} %get-tuple-element.44.bias_ref, bf16[128,1024]{1,0:T(8,128)(2,1)S(1)} %get-tuple-element.45.q_ref, ...), custom_call_target="tpu_custom_call" | custom-call | tf_op jit(solution)/shard_map/attention_backward/pallas_call | solution.py:190
  19.5 0.6 %collective-permute-start.10 = (bf16[2,128,256]{2,1,0:T(8,128)(2,1)S(1)}, bf16[2,128,256]{2,1,0:T(8,128)(2,1)S(1)}, u32[]{:S(2)}, u32[]{:S(2)}) collective-permute-start(bf16[2,128,256]{2,1,0:T(8,128)(2,1)S(1)} %get-tuple-element.61), channel_id=1, source_target_pairs={{0,7},{1,0},{2,1},{3,2},{4,3},{5,4},{6,5},{7,6},{8,15},{9,8},{10,9... | collective-permute-start | bytes 393224 | tf_op jit(solution)/shard_map/ppermute | solution.py:31
  20.1 0.1 collective-permute-done.6.prev_ref
  20.2 0.7 %attention_backward.7 = (bf16[128,1024]{1,0:T(8,128)(2,1)S(1)}, f32[2,128,256]{2,1,0:T(8,128)S(1)}, bf16[2,128,256]{2,1,0:T(8,128)(2,1)S(1)}) custom-call(f32[8,128]{1,0:T(8,128)S(1)} %get-tuple-element.48.bias_ref, bf16[128,1024]{1,0:T(8,128)(2,1)S(1)} %get-tuple-element.49.q_ref, bf16[128,1024]{1,0:T(8,128)(2,1)S(1)} %get-tuple-element.50.g_ref, ...), custom_call_target="tpu_custom_call" | custom-call | tf_op jit(solution)/shard_map/attention_backward/pallas_call | solution.py:190
  20.9 1.8 %collective-permute-start.12 = (bf16[2,128,256]{2,1,0:T(8,128)(2,1)S(1)}, bf16[2,128,256]{2,1,0:T(8,128)(2,1)S(1)}, u32[]{:S(2)}, u32[]{:S(2)}) collective-permute-start(bf16[2,128,256]{2,1,0:T(8,128)(2,1)S(1)} %get-tuple-element.63), channel_id=1, source_target_pairs={{0,7},{1,0},{2,1},{3,2},{4,3},{5,4},{6,5},{7,6},{8,15},{9,8},{10,9... | collective-permute-start | bytes 393224 | tf_op jit(solution)/shard_map/ppermute | solution.py:31
  22.7 0.0 collective-permute-done.8
  22.7 0.0 collective-permute-done.7
  22.7 2.3 %collective-permute-start.9 = (bf16[2,128,256]{2,1,0:T(8,128)(2,1)S(1)}, bf16[2,128,256]{2,1,0:T(8,128)(2,1)S(1)}, u32[]{:S(2)}, u32[]{:S(2)}) collective-permute-start(bf16[2,128,256]{2,1,0:T(8,128)(2,1)S(1)} %add_convert_fusion.2), channel_id=1, source_target_pairs={{0,24},{1,25},{2,26},{3,27},{4,28},{5,29},{6,30},{7,31},{8,16},{9,... | collective-permute-start | bytes 393224 | tf_op jit(solution)/shard_map/ppermute | solution.py:31
  25.1 0.0 collective-permute-done.10
  25.1 0.8 %collective-permute-start.11 = (bf16[2,128,256]{2,1,0:T(8,128)(2,1)S(1)}, bf16[2,128,256]{2,1,0:T(8,128)(2,1)S(1)}, u32[]{:S(2)}, u32[]{:S(2)}) collective-permute-start(bf16[2,128,256]{2,1,0:T(8,128)(2,1)S(1)} %add_convert_fusion.1), channel_id=1, source_target_pairs={{0,16},{1,17},{2,18},{3,19},{4,20},{5,21},{6,22},{7,23},{8,24},{9,... | collective-permute-start | bytes 393224 | tf_op jit(solution)/shard_map/ppermute | solution.py:31
  25.9 0.0 collective-permute-done.12
  25.9 0.9 %collective-permute-start.13 = (bf16[2,128,256]{2,1,0:T(8,128)(2,1)S(1)}, bf16[2,128,256]{2,1,0:T(8,128)(2,1)S(1)}, u32[]{:S(2)}, u32[]{:S(2)}) collective-permute-start(bf16[2,128,256]{2,1,0:T(8,128)(2,1)S(1)} %add_convert_fusion), channel_id=1, source_target_pairs={{0,8},{1,9},{2,10},{3,11},{4,12},{5,13},{6,14},{7,15},{8,0},{9,1},... | collective-permute-start | bytes 393224 | tf_op jit(solution)/shard_map/ppermute | solution.py:31
  26.8 1.0 %store_slices.1 = bf16[128,4096]{1,0:T(8,128)(2,1)} custom-call(bf16[128,1024]{1,0:T(8,128)(2,1)S(1)} %get-tuple-element.38.refs_0_, bf16[128,1024]{1,0:T(8,128)(2,1)S(1)} %get-tuple-element.52.refs_1_, bf16[128,1024]{1,0:T(8,128)(2,1)S(1)} %get-tuple-element.53.refs_2_, bf16[128,1024]{1,0:T(8,128)(2,1)S(1)} %get-tuple-element.54.refs_3_), custom_call_target="tpu_custom_call" | custom-call | tf_op jit(solution)/shard_map/store_slices/pallas_call | solution.py:220
  27.9 1.3 %collective-permute-done.9 = bf16[2,128,256]{2,1,0:T(8,128)(2,1)S(1)} collective-permute-done((bf16[2,128,256]{2,1,0:T(8,128)(2,1)S(1)}, bf16[2,128,256]{2,1,0:T(8,128)(2,1)S(1)}, u32[]{:S(2)}, u32[]{:S(2)}) %collective-permute-start.9) | collective-permute-done | bytes 131104 | tf_op jit(solution)/shard_map/ppermute | solution.py:31
  29.2 2.7 %collective-permute-done.11 = bf16[2,128,256]{2,1,0:T(8,128)(2,1)S(1)} collective-permute-done((bf16[2,128,256]{2,1,0:T(8,128)(2,1)S(1)}, bf16[2,128,256]{2,1,0:T(8,128)(2,1)S(1)}, u32[]{:S(2)}, u32[]{:S(2)}) %collective-permute-start.11) | collective-permute-done | bytes 131104 | tf_op jit(solution)/shard_map/ppermute | solution.py:31
  31.9 0.0 collective-permute-done.13
  31.9 0.1 add_add_fusion
  32.0 0.7 %slice_bitcast_fusion = (f32[128,256]{1,0:T(8,128)}, f32[128,256]{1,0:T(8,128)}) fusion(f32[2,128,256]{2,1,0:T(8,128)S(1)} %add_add_fusion), kind=kLoop, calls=%fused_computation.4 | loop fusion | bytes 524288 | tf_op jit(solution)/shard_map/squeeze | solution.py:229
  (3 shorter events, 0.1 us)
Async XLA Ops:
  1.5 7.5 %collective-permute-start = (bf16[2,128,256]{2,1,0:T(8,128)(2,1)S(1)}, bf16[2,128,256]{2,1,0:T(8,128)(2,1)S(1)}, u32[]{:S(2)}, u32[]{:S(2)}) collective-permute-start(bf16[2,128,256]{2,1,0:T(8,128)(2,1)S(1)} %pad_maximum_fusion.own_ref), channel_id=1, source_target_pairs={{0,24},{1,25},{2,26},{3,27},{4,28},{5,29},{6,30},{7,31},{8,16},{9,... | collective-permute-start | bytes 393224 | tf_op jit(solution)/shard_map/ppermute | solution.py:31
  5.5 6.2 %collective-permute-start.1 = (bf16[2,128,256]{2,1,0:T(8,128)(2,1)S(1)}, bf16[2,128,256]{2,1,0:T(8,128)(2,1)S(1)}, u32[]{:S(2)}, u32[]{:S(2)}) collective-permute-start(bf16[2,128,256]{2,1,0:T(8,128)(2,1)S(1)} %pad_maximum_fusion.own_ref), channel_id=1, source_target_pairs={{0,1},{1,2},{2,3},{3,4},{4,5},{5,6},{6,7},{7,0},{8,9},{9,10},{10,1... | collective-permute-start | bytes 393224 | tf_op jit(solution)/shard_map/ppermute | solution.py:31
  5.5 6.9 %collective-permute-start.2 = (bf16[2,128,256]{2,1,0:T(8,128)(2,1)S(1)}, bf16[2,128,256]{2,1,0:T(8,128)(2,1)S(1)}, u32[]{:S(2)}, u32[]{:S(2)}) collective-permute-start(bf16[2,128,256]{2,1,0:T(8,128)(2,1)S(1)} %pad_maximum_fusion.own_ref), channel_id=1, source_target_pairs={{0,16},{1,17},{2,18},{3,19},{4,20},{5,21},{6,22},{7,23},{8,24},{9,... | collective-permute-start | bytes 393224 | tf_op jit(solution)/shard_map/ppermute | solution.py:31
  6.0 6.4 %collective-permute-start.3 = (bf16[2,128,256]{2,1,0:T(8,128)(2,1)S(1)}, bf16[2,128,256]{2,1,0:T(8,128)(2,1)S(1)}, u32[]{:S(2)}, u32[]{:S(2)}) collective-permute-start(bf16[2,128,256]{2,1,0:T(8,128)(2,1)S(1)} %pad_maximum_fusion.own_ref), channel_id=1, source_target_pairs={{0,8},{1,9},{2,10},{3,11},{4,12},{5,13},{6,14},{7,15},{8,0},{9,1},... | collective-permute-start | bytes 393224 | tf_op jit(solution)/shard_map/ppermute | solution.py:31
  9.0 6.2 %collective-permute-start.4 = (bf16[2,128,256]{2,1,0:T(8,128)(2,1)S(1)}, bf16[2,128,256]{2,1,0:T(8,128)(2,1)S(1)}, u32[]{:S(2)}, u32[]{:S(2)}) collective-permute-start(bf16[2,128,256]{2,1,0:T(8,128)(2,1)S(1)} %collective-permute-done.own_ref), channel_id=1, source_target_pairs={{0,1},{1,2},{2,3},{3,4},{4,5},{5,6},{6,7},{7,0},{8,9},{9,10},{10,1... | collective-permute-start | bytes 393224 | tf_op jit(solution)/shard_map/ppermute | solution.py:31
  12.4 6.4 %collective-permute-start.5 = (bf16[2,128,256]{2,1,0:T(8,128)(2,1)S(1)}, bf16[2,128,256]{2,1,0:T(8,128)(2,1)S(1)}, u32[]{:S(2)}, u32[]{:S(2)}) collective-permute-start(bf16[2,128,256]{2,1,0:T(8,128)(2,1)S(1)} %collective-permute-done.2.own_ref), channel_id=1, source_target_pairs={{0,1},{1,2},{2,3},{3,4},{4,5},{5,6},{6,7},{7,0},{8,9},{9,10},{10,1... | collective-permute-start | bytes 393224 | tf_op jit(solution)/shard_map/ppermute | solution.py:31
  12.5 7.7 %collective-permute-start.6 = (bf16[2,128,256]{2,1,0:T(8,128)(2,1)S(1)}, bf16[2,128,256]{2,1,0:T(8,128)(2,1)S(1)}, u32[]{:S(2)}, u32[]{:S(2)}) collective-permute-start(bf16[2,128,256]{2,1,0:T(8,128)(2,1)S(1)} %collective-permute-done.3.own_ref), channel_id=1, source_target_pairs={{0,1},{1,2},{2,3},{3,4},{4,5},{5,6},{6,7},{7,0},{8,9},{9,10},{10,1... | collective-permute-start | bytes 393224 | tf_op jit(solution)/shard_map/ppermute | solution.py:31
  15.9 6.8 %collective-permute-start.8 = (bf16[2,128,256]{2,1,0:T(8,128)(2,1)S(1)}, bf16[2,128,256]{2,1,0:T(8,128)(2,1)S(1)}, u32[]{:S(2)}, u32[]{:S(2)}) collective-permute-start(bf16[2,128,256]{2,1,0:T(8,128)(2,1)S(1)} %get-tuple-element.58), channel_id=1, source_target_pairs={{0,7},{1,0},{2,1},{3,2},{4,3},{5,4},{6,5},{7,6},{8,15},{9,8},{10,9... | collective-permute-start | bytes 393224 | tf_op jit(solution)/shard_map/ppermute | solution.py:31
  17.4 5.3 %collective-permute-start.7 = (bf16[2,128,256]{2,1,0:T(8,128)(2,1)S(1)}, bf16[2,128,256]{2,1,0:T(8,128)(2,1)S(1)}, u32[]{:S(2)}, u32[]{:S(2)}) collective-permute-start(bf16[2,128,256]{2,1,0:T(8,128)(2,1)S(1)} %get-tuple-element.56), channel_id=1, source_target_pairs={{0,7},{1,0},{2,1},{3,2},{4,3},{5,4},{6,5},{7,6},{8,15},{9,8},{10,9... | collective-permute-start | bytes 393224 | tf_op jit(solution)/shard_map/ppermute | solution.py:31
  19.5 5.6 %collective-permute-start.10 = (bf16[2,128,256]{2,1,0:T(8,128)(2,1)S(1)}, bf16[2,128,256]{2,1,0:T(8,128)(2,1)S(1)}, u32[]{:S(2)}, u32[]{:S(2)}) collective-permute-start(bf16[2,128,256]{2,1,0:T(8,128)(2,1)S(1)} %get-tuple-element.61), channel_id=1, source_target_pairs={{0,7},{1,0},{2,1},{3,2},{4,3},{5,4},{6,5},{7,6},{8,15},{9,8},{10,9... | collective-permute-start | bytes 393224 | tf_op jit(solution)/shard_map/ppermute | solution.py:31
  20.9 5.0 %collective-permute-start.12 = (bf16[2,128,256]{2,1,0:T(8,128)(2,1)S(1)}, bf16[2,128,256]{2,1,0:T(8,128)(2,1)S(1)}, u32[]{:S(2)}, u32[]{:S(2)}) collective-permute-start(bf16[2,128,256]{2,1,0:T(8,128)(2,1)S(1)} %get-tuple-element.63), channel_id=1, source_target_pairs={{0,7},{1,0},{2,1},{3,2},{4,3},{5,4},{6,5},{7,6},{8,15},{9,8},{10,9... | collective-permute-start | bytes 393224 | tf_op jit(solution)/shard_map/ppermute | solution.py:31
  22.7 6.5 %collective-permute-start.9 = (bf16[2,128,256]{2,1,0:T(8,128)(2,1)S(1)}, bf16[2,128,256]{2,1,0:T(8,128)(2,1)S(1)}, u32[]{:S(2)}, u32[]{:S(2)}) collective-permute-start(bf16[2,128,256]{2,1,0:T(8,128)(2,1)S(1)} %add_convert_fusion.2), channel_id=1, source_target_pairs={{0,24},{1,25},{2,26},{3,27},{4,28},{5,29},{6,30},{7,31},{8,16},{9,... | collective-permute-start | bytes 393224 | tf_op jit(solution)/shard_map/ppermute | solution.py:31
  25.1 6.8 %collective-permute-start.11 = (bf16[2,128,256]{2,1,0:T(8,128)(2,1)S(1)}, bf16[2,128,256]{2,1,0:T(8,128)(2,1)S(1)}, u32[]{:S(2)}, u32[]{:S(2)}) collective-permute-start(bf16[2,128,256]{2,1,0:T(8,128)(2,1)S(1)} %add_convert_fusion.1), channel_id=1, source_target_pairs={{0,16},{1,17},{2,18},{3,19},{4,20},{5,21},{6,22},{7,23},{8,24},{9,... | collective-permute-start | bytes 393224 | tf_op jit(solution)/shard_map/ppermute | solution.py:31
  25.9 6.0 %collective-permute-start.13 = (bf16[2,128,256]{2,1,0:T(8,128)(2,1)S(1)}, bf16[2,128,256]{2,1,0:T(8,128)(2,1)S(1)}, u32[]{:S(2)}, u32[]{:S(2)}) collective-permute-start(bf16[2,128,256]{2,1,0:T(8,128)(2,1)S(1)} %add_convert_fusion), channel_id=1, source_target_pairs={{0,8},{1,9},{2,10},{3,11},{4,12},{5,13},{6,14},{7,15},{8,0},{9,1},... | collective-permute-start | bytes 393224 | tf_op jit(solution)/shard_map/ppermute | solution.py:31

commit v2 on v0

--- a/solution.py
+++ b/solution.py
@@ -183,6 +183,7 @@
     )
     bias = loaded[-1]
     prev[order[1]] = rotate_seq(after(own[order[1]], bias), 1)
+    prev[order[-1]] = swap_section(prev[0], order[-1])
     bias = after(bias, own[order[1]])
     total, dq_parts, own_grads, back = None, {}, {}, {}
     for step, flip in enumerate(order):
@@ -203,7 +204,7 @@
         bias = out[0]
         if step == 0:
             back[0] = rotate_seq(held, -1)
-            for later in order[2:]:
+            for later in order[2:-1]:
                 prev[later] = rotate_seq(after(own[later], bias), 1)
             bias = after(bias, [own[later] for later in order])
         else:

time: 32.7 us -> 32.7 us (level)
  starting transfers between devices: 15.6 us -> 17.5 us
  waiting for transfers between devices: 8.28 us -> 6.4 us
    ppermute x14, starting transfers between devices: 15.6 us -> 17.5 us  [exchanged(): return lax.ppermute(x, ('section', 'seq'), pairs)]
    ppermute x14, waiting for transfers between devices: 8.28 us -> 6.4 us  [exchanged(): return lax.ppermute(x, ('section', 'seq'), pairs)]
  transfers between devices with their start and end apart: 14 -> 14, of which waited for: 6 -> 5; matrix products, arithmetic and copies ran while one was open for 0% -> 0% of each run, Pallas kernels for 17% -> 17%
where the time goes in v2:
time: 32.7 us; the launch traced here: 32.5 us
  starting transfers between devices  17.5 us (54%)
  waiting for transfers between devices  6.4 us (20%)
  Pallas kernels  5.44 us (17%)
  between operations  1.39 us (4%)
  other arithmetic  1.06 us (3%)
  local copies, waits for them, and re-layouts  0.72 us (2%)
    ppermute x14, starting transfers between devices, exchanged(): return lax.ppermute(x, ('section', 'seq'), pairs)  17.5 us
    ppermute x14, waiting for transfers between devices, exchanged(): return lax.ppermute(x, ('section', 'seq'), pairs)  6.4 us
    pallas_call x4, Pallas kernels, body(): pl.pallas_call(attention_kernel, out_shape=[tile] * (not last) + [q_slice...  2.85 us
    pallas_call x1, Pallas kernels, body(): pl.pallas_call(functools.partial(load_kernel, slices), out_shape=[q_slice...  1.59 us
    pallas_call x1, Pallas kernels, body(): pl.pallas_call(functools.partial(store_kernel, slices), out_shape=jax.Sha...  0.99 us
    another operation x1, other arithmetic, body(): pair = jnp.stack([keys, values])  0.89 us
    squeeze x1, local copies, waits for them, and re-layouts, body(): return (dq[None], total[0], total[1])  0.72 us
  transfers between devices with their start and end apart: 14, of which 5 were waited for; matrix products, arithmetic and copies ran while one was open for 0% of the time, Pallas kernels for 17%

profile of v2, /device:TPU:0, one launch (start us, length us, event | category | flops | bytes accessed | tf_op | source)
XLA Modules:
  0.0 32.5 jit_solution(6171392942187021622)
XLA Ops:
  0.6 0.9 %pad_maximum_fusion.own_ref = bf16[2,128,256]{2,1,0:T(8,128)(2,1)S(1)} fusion(bf16[1,128,256]{2,1,0:T(8,128)(2,1)} %bitcast.12, bf16[1,128,256]{2,1,0:T(8,128)(2,1)} %bitcast.13), kind=kLoop, calls=%fused_computation.6 | loop fusion | flops 65536 | bytes 262144 | tf_op jit(solution)/shard_map/stack | solution.py:167
  1.5 4.0 %collective-permute-start = (bf16[2,128,256]{2,1,0:T(8,128)(2,1)S(1)}, bf16[2,128,256]{2,1,0:T(8,128)(2,1)S(1)}, u32[]{:S(2)}, u32[]{:S(2)}) collective-permute-start(bf16[2,128,256]{2,1,0:T(8,128)(2,1)S(1)} %pad_maximum_fusion.own_ref), channel_id=1, source_target_pairs={{0,24},{1,25},{2,26},{3,27},{4,28},{5,29},{6,30},{7,31},{8,16},{9,... | collective-permute-start | bytes 393224 | tf_op jit(solution)/shard_map/ppermute | solution.py:31
  5.5 0.0 collective-permute-start.1
  5.5 0.5 %collective-permute-start.2 = (bf16[2,128,256]{2,1,0:T(8,128)(2,1)S(1)}, bf16[2,128,256]{2,1,0:T(8,128)(2,1)S(1)}, u32[]{:S(2)}, u32[]{:S(2)}) collective-permute-start(bf16[2,128,256]{2,1,0:T(8,128)(2,1)S(1)} %pad_maximum_fusion.own_ref), channel_id=1, source_target_pairs={{0,16},{1,17},{2,18},{3,19},{4,20},{5,21},{6,22},{7,23},{8,24},{9,... | collective-permute-start | bytes 393224 | tf_op jit(solution)/shard_map/ppermute | solution.py:31
  6.0 0.2 collective-permute-start.3
  6.8 1.6 %load_slices.1 = (bf16[128,1024]{1,0:T(8,128)(2,1)S(1)}, bf16[128,1024]{1,0:T(8,128)(2,1)S(1)}, bf16[128,1024]{1,0:T(8,128)(2,1)S(1)}, bf16[128,1024]{1,0:T(8,12...) custom-call(s32[1]{0:T(128)S(6)} %copy.8.first_ref, ...), custom_call_target="tpu_custom_call" | custom-call | tf_op jit(solution)/shard_map/load_slices/pallas_call | solution.py:171
  8.4 0.5 %collective-permute-done.own_ref = bf16[2,128,256]{2,1,0:T(8,128)(2,1)S(1)} collective-permute-done((bf16[2,128,256]{2,1,0:T(8,128)(2,1)S(1)}, bf16[2,128,256]{2,1,0:T(8,128)(2,1)S(1)}, u32[]{:S(2)}, u32[]{:S(2)}) %collective-permute-start) | collective-permute-done | bytes 131104 | tf_op jit(solution)/shard_map/ppermute | solution.py:31
  9.0 1.0 %collective-permute-start.4 = (bf16[2,128,256]{2,1,0:T(8,128)(2,1)S(1)}, bf16[2,128,256]{2,1,0:T(8,128)(2,1)S(1)}, u32[]{:S(2)}, u32[]{:S(2)}) collective-permute-start(bf16[2,128,256]{2,1,0:T(8,128)(2,1)S(1)} %collective-permute-done.own_ref), channel_id=1, source_target_pairs={{0,1},{1,2},{2,3},{3,4},{4,5},{5,6},{6,7},{7,0},{8,9},{9,10},{10,1... | collective-permute-start | bytes 393224 | tf_op jit(solution)/shard_map/ppermute | solution.py:31
  10.0 1.7 %collective-permute-done.1.prev_ref = bf16[2,128,256]{2,1,0:T(8,128)(2,1)S(1)} collective-permute-done((bf16[2,128,256]{2,1,0:T(8,128)(2,1)S(1)}, bf16[2,128,256]{2,1,0:T(8,128)(2,1)S(1)}, u32[]{:S(2)}, u32[]{:S(2)}) %collective-permute-start.1) | collective-permute-done | bytes 131104 | tf_op jit(solution)/shard_map/ppermute | solution.py:31
  11.7 0.7 %attention_backward.4 = (f32[8,128]{1,0:T(8,128)S(1)}, bf16[128,1024]{1,0:T(8,128)(2,1)S(1)}, f32[2,128,256]{2,1,0:T(8,128)S(1)}, bf16[2,128,256]{2,1,0:T(8,128)(2,1)S(1)}) custom-call(f32[8,128]{1,0:T(8,128)S(1)} %get-tuple-element.33.bias_ref, bf16[128,1024]{1,0:T(8,128)(2,1)S(1)} %get-tuple-element.34.q_ref, ...), custom_call_target="tpu_custom_call" | custom-call | tf_op jit(solution)/shard_map/attention_backward/pallas_call | solution.py:191
  12.4 0.0 collective-permute-done.2.own_ref
  12.4 0.1 collective-permute-start.5
  12.5 0.0 collective-permute-done.3.own_ref
  12.5 1.3 %collective-permute-start.6 = (bf16[2,128,256]{2,1,0:T(8,128)(2,1)S(1)}, bf16[2,128,256]{2,1,0:T(8,128)(2,1)S(1)}, u32[]{:S(2)}, u32[]{:S(2)}) collective-permute-start(bf16[2,128,256]{2,1,0:T(8,128)(2,1)S(1)} %collective-permute-done.1.prev_ref), channel_id=1, source_target_pairs={{0,8},{1,9},{2,10},{3,11},{4,12},{5,13},{6,14},{7,15},{8,0},{9,1},... | collective-permute-start | bytes 393224 | tf_op jit(solution)/shard_map/ppermute | solution.py:31
  13.7 2.9 %collective-permute-start.8 = (bf16[2,128,256]{2,1,0:T(8,128)(2,1)S(1)}, bf16[2,128,256]{2,1,0:T(8,128)(2,1)S(1)}, u32[]{:S(2)}, u32[]{:S(2)}) collective-permute-start(bf16[2,128,256]{2,1,0:T(8,128)(2,1)S(1)} %get-tuple-element.54), channel_id=1, source_target_pairs={{0,7},{1,0},{2,1},{3,2},{4,3},{5,4},{6,5},{7,6},{8,15},{9,8},{10,9... | collective-permute-start | bytes 393224 | tf_op jit(solution)/shard_map/ppermute | solution.py:31
  16.7 0.0 collective-permute-done.4.prev_ref
  16.7 0.7 %attention_backward.5 = (f32[8,128]{1,0:T(8,128)S(1)}, bf16[128,1024]{1,0:T(8,128)(2,1)S(1)}, f32[2,128,256]{2,1,0:T(8,128)S(1)}, bf16[2,128,256]{2,1,0:T(8,128)(2,1)S(1)}) custom-call(f32[8,128]{1,0:T(8,128)S(1)} %get-tuple-element.38.bias_ref, bf16[128,1024]{1,0:T(8,128)(2,1)S(1)} %get-tuple-element.39.q_ref, ...), custom_call_target="tpu_custom_call" | custom-call | tf_op jit(solution)/shard_map/attention_backward/pallas_call | solution.py:191
  17.4 1.2 %collective-permute-start.7 = (bf16[2,128,256]{2,1,0:T(8,128)(2,1)S(1)}, bf16[2,128,256]{2,1,0:T(8,128)(2,1)S(1)}, u32[]{:S(2)}, u32[]{:S(2)}) collective-permute-start(bf16[2,128,256]{2,1,0:T(8,128)(2,1)S(1)} %get-tuple-element.53), channel_id=1, source_target_pairs={{0,7},{1,0},{2,1},{3,2},{4,3},{5,4},{6,5},{7,6},{8,15},{9,8},{10,9... | collective-permute-start | bytes 393224 | tf_op jit(solution)/shard_map/ppermute | solution.py:31
  18.6 0.1 collective-permute-done.5.prev_ref
  18.7 0.7 %attention_backward.6 = (f32[8,128]{1,0:T(8,128)S(1)}, bf16[128,1024]{1,0:T(8,128)(2,1)S(1)}, f32[2,128,256]{2,1,0:T(8,128)S(1)}, bf16[2,128,256]{2,1,0:T(8,128)(2,1)S(1)}) custom-call(f32[8,128]{1,0:T(8,128)S(1)} %get-tuple-element.42.bias_ref, bf16[128,1024]{1,0:T(8,128)(2,1)S(1)} %get-tuple-element.43.q_ref, ...), custom_call_target="tpu_custom_call" | custom-call | tf_op jit(solution)/shard_map/attention_backward/pallas_call | solution.py:191
  19.4 1.8 %collective-permute-start.10 = (bf16[2,128,256]{2,1,0:T(8,128)(2,1)S(1)}, bf16[2,128,256]{2,1,0:T(8,128)(2,1)S(1)}, u32[]{:S(2)}, u32[]{:S(2)}) collective-permute-start(bf16[2,128,256]{2,1,0:T(8,128)(2,1)S(1)} %get-tuple-element.57), channel_id=1, source_target_pairs={{0,7},{1,0},{2,1},{3,2},{4,3},{5,4},{6,5},{7,6},{8,15},{9,8},{10,9... | collective-permute-start | bytes 393224 | tf_op jit(solution)/shard_map/ppermute | solution.py:31
  21.2 0.0 collective-permute-done.6.prev_ref
  21.2 0.7 %attention_backward.7 = (bf16[128,1024]{1,0:T(8,128)(2,1)S(1)}, f32[2,128,256]{2,1,0:T(8,128)S(1)}, bf16[2,128,256]{2,1,0:T(8,128)(2,1)S(1)}) custom-call(f32[8,128]{1,0:T(8,128)S(1)} %get-tuple-element.46.bias_ref, bf16[128,1024]{1,0:T(8,128)(2,1)S(1)} %get-tuple-element.47.q_ref, bf16[128,1024]{1,0:T(8,128)(2,1)S(1)} %get-tuple-element.48.g_ref, ...), custom_call_target="tpu_custom_call" | custom-call | tf_op jit(solution)/shard_map/attention_backward/pallas_call | solution.py:191
  21.9 0.7 %collective-permute-start.12 = (bf16[2,128,256]{2,1,0:T(8,128)(2,1)S(1)}, bf16[2,128,256]{2,1,0:T(8,128)(2,1)S(1)}, u32[]{:S(2)}, u32[]{:S(2)}) collective-permute-start(bf16[2,128,256]{2,1,0:T(8,128)(2,1)S(1)} %get-tuple-element.59), channel_id=1, source_target_pairs={{0,7},{1,0},{2,1},{3,2},{4,3},{5,4},{6,5},{7,6},{8,15},{9,8},{10,9... | collective-permute-start | bytes 393224 | tf_op jit(solution)/shard_map/ppermute | solution.py:31
  22.6 0.0 collective-permute-done.8
  22.6 0.0 collective-permute-done.7
  22.7 2.4 %collective-permute-start.9 = (bf16[2,128,256]{2,1,0:T(8,128)(2,1)S(1)}, bf16[2,128,256]{2,1,0:T(8,128)(2,1)S(1)}, u32[]{:S(2)}, u32[]{:S(2)}) collective-permute-start(bf16[2,128,256]{2,1,0:T(8,128)(2,1)S(1)} %add_convert_fusion.2), channel_id=1, source_target_pairs={{0,24},{1,25},{2,26},{3,27},{4,28},{5,29},{6,30},{7,31},{8,16},{9,... | collective-permute-start | bytes 393224 | tf_op jit(solution)/shard_map/ppermute | solution.py:31
  25.0 0.0 collective-permute-done.10
  25.1 0.7 %collective-permute-start.11 = (bf16[2,128,256]{2,1,0:T(8,128)(2,1)S(1)}, bf16[2,128,256]{2,1,0:T(8,128)(2,1)S(1)}, u32[]{:S(2)}, u32[]{:S(2)}) collective-permute-start(bf16[2,128,256]{2,1,0:T(8,128)(2,1)S(1)} %add_convert_fusion.1), channel_id=1, source_target_pairs={{0,16},{1,17},{2,18},{3,19},{4,20},{5,21},{6,22},{7,23},{8,24},{9,... | collective-permute-start | bytes 393224 | tf_op jit(solution)/shard_map/ppermute | solution.py:31
  25.8 0.0 collective-permute-done.12
  25.8 0.9 %collective-permute-start.13 = (bf16[2,128,256]{2,1,0:T(8,128)(2,1)S(1)}, bf16[2,128,256]{2,1,0:T(8,128)(2,1)S(1)}, u32[]{:S(2)}, u32[]{:S(2)}) collective-permute-start(bf16[2,128,256]{2,1,0:T(8,128)(2,1)S(1)} %add_convert_fusion), channel_id=1, source_target_pairs={{0,8},{1,9},{2,10},{3,11},{4,12},{5,13},{6,14},{7,15},{8,0},{9,1},... | collective-permute-start | bytes 393224 | tf_op jit(solution)/shard_map/ppermute | solution.py:31
  26.8 1.0 %store_slices.1 = bf16[128,4096]{1,0:T(8,128)(2,1)} custom-call(bf16[128,1024]{1,0:T(8,128)(2,1)S(1)} %get-tuple-element.36.refs_0_, bf16[128,1024]{1,0:T(8,128)(2,1)S(1)} %get-tuple-element.49.refs_1_, bf16[128,1024]{1,0:T(8,128)(2,1)S(1)} %get-tuple-element.50.refs_2_, bf16[128,1024]{1,0:T(8,128)(2,1)S(1)} %get-tuple-element.51.refs_3_), custom_call_target="tpu_custom_call" | custom-call | tf_op jit(solution)/shard_map/store_slices/pallas_call | solution.py:219
  27.8 1.2 %collective-permute-done.9 = bf16[2,128,256]{2,1,0:T(8,128)(2,1)S(1)} collective-permute-done((bf16[2,128,256]{2,1,0:T(8,128)(2,1)S(1)}, bf16[2,128,256]{2,1,0:T(8,128)(2,1)S(1)}, u32[]{:S(2)}, u32[]{:S(2)}) %collective-permute-start.9) | collective-permute-done | bytes 131104 | tf_op jit(solution)/shard_map/ppermute | solution.py:31
  29.0 2.7 %collective-permute-done.11 = bf16[2,128,256]{2,1,0:T(8,128)(2,1)S(1)} collective-permute-done((bf16[2,128,256]{2,1,0:T(8,128)(2,1)S(1)}, bf16[2,128,256]{2,1,0:T(8,128)(2,1)S(1)}, u32[]{:S(2)}, u32[]{:S(2)}) %collective-permute-start.11) | collective-permute-done | bytes 131104 | tf_op jit(solution)/shard_map/ppermute | solution.py:31
  31.7 0.0 collective-permute-done.13
  31.7 0.1 add_add_fusion
  31.8 0.7 %slice_bitcast_fusion = (f32[128,256]{1,0:T(8,128)}, f32[128,256]{1,0:T(8,128)}) fusion(f32[2,128,256]{2,1,0:T(8,128)S(1)} %add_add_fusion), kind=kLoop, calls=%fused_computation.4 | loop fusion | bytes 524288 | tf_op jit(solution)/shard_map/squeeze | solution.py:228
  (3 shorter events, 0.1 us)
Async XLA Ops:
  1.5 7.5 %collective-permute-start = (bf16[2,128,256]{2,1,0:T(8,128)(2,1)S(1)}, bf16[2,128,256]{2,1,0:T(8,128)(2,1)S(1)}, u32[]{:S(2)}, u32[]{:S(2)}) collective-permute-start(bf16[2,128,256]{2,1,0:T(8,128)(2,1)S(1)} %pad_maximum_fusion.own_ref), channel_id=1, source_target_pairs={{0,24},{1,25},{2,26},{3,27},{4,28},{5,29},{6,30},{7,31},{8,16},{9,... | collective-permute-start | bytes 393224 | tf_op jit(solution)/shard_map/ppermute | solution.py:31
  5.5 6.2 %collective-permute-start.1 = (bf16[2,128,256]{2,1,0:T(8,128)(2,1)S(1)}, bf16[2,128,256]{2,1,0:T(8,128)(2,1)S(1)}, u32[]{:S(2)}, u32[]{:S(2)}) collective-permute-start(bf16[2,128,256]{2,1,0:T(8,128)(2,1)S(1)} %pad_maximum_fusion.own_ref), channel_id=1, source_target_pairs={{0,1},{1,2},{2,3},{3,4},{4,5},{5,6},{6,7},{7,0},{8,9},{9,10},{10,1... | collective-permute-start | bytes 393224 | tf_op jit(solution)/shard_map/ppermute | solution.py:31
  5.5 6.9 %collective-permute-start.2 = (bf16[2,128,256]{2,1,0:T(8,128)(2,1)S(1)}, bf16[2,128,256]{2,1,0:T(8,128)(2,1)S(1)}, u32[]{:S(2)}, u32[]{:S(2)}) collective-permute-start(bf16[2,128,256]{2,1,0:T(8,128)(2,1)S(1)} %pad_maximum_fusion.own_ref), channel_id=1, source_target_pairs={{0,16},{1,17},{2,18},{3,19},{4,20},{5,21},{6,22},{7,23},{8,24},{9,... | collective-permute-start | bytes 393224 | tf_op jit(solution)/shard_map/ppermute | solution.py:31
  6.0 6.5 %collective-permute-start.3 = (bf16[2,128,256]{2,1,0:T(8,128)(2,1)S(1)}, bf16[2,128,256]{2,1,0:T(8,128)(2,1)S(1)}, u32[]{:S(2)}, u32[]{:S(2)}) collective-permute-start(bf16[2,128,256]{2,1,0:T(8,128)(2,1)S(1)} %pad_maximum_fusion.own_ref), channel_id=1, source_target_pairs={{0,8},{1,9},{2,10},{3,11},{4,12},{5,13},{6,14},{7,15},{8,0},{9,1},... | collective-permute-start | bytes 393224 | tf_op jit(solution)/shard_map/ppermute | solution.py:31
  9.0 7.7 %collective-permute-start.4 = (bf16[2,128,256]{2,1,0:T(8,128)(2,1)S(1)}, bf16[2,128,256]{2,1,0:T(8,128)(2,1)S(1)}, u32[]{:S(2)}, u32[]{:S(2)}) collective-permute-start(bf16[2,128,256]{2,1,0:T(8,128)(2,1)S(1)} %collective-permute-done.own_ref), channel_id=1, source_target_pairs={{0,1},{1,2},{2,3},{3,4},{4,5},{5,6},{6,7},{7,0},{8,9},{9,10},{10,1... | collective-permute-start | bytes 393224 | tf_op jit(solution)/shard_map/ppermute | solution.py:31
  12.4 6.3 %collective-permute-start.5 = (bf16[2,128,256]{2,1,0:T(8,128)(2,1)S(1)}, bf16[2,128,256]{2,1,0:T(8,128)(2,1)S(1)}, u32[]{:S(2)}, u32[]{:S(2)}) collective-permute-start(bf16[2,128,256]{2,1,0:T(8,128)(2,1)S(1)} %collective-permute-done.2.own_ref), channel_id=1, source_target_pairs={{0,1},{1,2},{2,3},{3,4},{4,5},{5,6},{6,7},{7,0},{8,9},{9,10},{10,1... | collective-permute-start | bytes 393224 | tf_op jit(solution)/shard_map/ppermute | solution.py:31
  12.5 8.7 %collective-permute-start.6 = (bf16[2,128,256]{2,1,0:T(8,128)(2,1)S(1)}, bf16[2,128,256]{2,1,0:T(8,128)(2,1)S(1)}, u32[]{:S(2)}, u32[]{:S(2)}) collective-permute-start(bf16[2,128,256]{2,1,0:T(8,128)(2,1)S(1)} %collective-permute-done.1.prev_ref), channel_id=1, source_target_pairs={{0,8},{1,9},{2,10},{3,11},{4,12},{5,13},{6,14},{7,15},{8,0},{9,1},... | collective-permute-start | bytes 393224 | tf_op jit(solution)/shard_map/ppermute | solution.py:31
  13.7 8.9 %collective-permute-start.8 = (bf16[2,128,256]{2,1,0:T(8,128)(2,1)S(1)}, bf16[2,128,256]{2,1,0:T(8,128)(2,1)S(1)}, u32[]{:S(2)}, u32[]{:S(2)}) collective-permute-start(bf16[2,128,256]{2,1,0:T(8,128)(2,1)S(1)} %get-tuple-element.54), channel_id=1, source_target_pairs={{0,7},{1,0},{2,1},{3,2},{4,3},{5,4},{6,5},{7,6},{8,15},{9,8},{10,9... | collective-permute-start | bytes 393224 | tf_op jit(solution)/shard_map/ppermute | solution.py:31
  17.4 5.2 %collective-permute-start.7 = (bf16[2,128,256]{2,1,0:T(8,128)(2,1)S(1)}, bf16[2,128,256]{2,1,0:T(8,128)(2,1)S(1)}, u32[]{:S(2)}, u32[]{:S(2)}) collective-permute-start(bf16[2,128,256]{2,1,0:T(8,128)(2,1)S(1)} %get-tuple-element.53), channel_id=1, source_target_pairs={{0,7},{1,0},{2,1},{3,2},{4,3},{5,4},{6,5},{7,6},{8,15},{9,8},{10,9... | collective-permute-start | bytes 393224 | tf_op jit(solution)/shard_map/ppermute | solution.py:31
  19.4 5.6 %collective-permute-start.10 = (bf16[2,128,256]{2,1,0:T(8,128)(2,1)S(1)}, bf16[2,128,256]{2,1,0:T(8,128)(2,1)S(1)}, u32[]{:S(2)}, u32[]{:S(2)}) collective-permute-start(bf16[2,128,256]{2,1,0:T(8,128)(2,1)S(1)} %get-tuple-element.57), channel_id=1, source_target_pairs={{0,7},{1,0},{2,1},{3,2},{4,3},{5,4},{6,5},{7,6},{8,15},{9,8},{10,9... | collective-permute-start | bytes 393224 | tf_op jit(solution)/shard_map/ppermute | solution.py:31
  21.9 3.9 %collective-permute-start.12 = (bf16[2,128,256]{2,1,0:T(8,128)(2,1)S(1)}, bf16[2,128,256]{2,1,0:T(8,128)(2,1)S(1)}, u32[]{:S(2)}, u32[]{:S(2)}) collective-permute-start(bf16[2,128,256]{2,1,0:T(8,128)(2,1)S(1)} %get-tuple-element.59), channel_id=1, source_target_pairs={{0,7},{1,0},{2,1},{3,2},{4,3},{5,4},{6,5},{7,6},{8,15},{9,8},{10,9... | collective-permute-start | bytes 393224 | tf_op jit(solution)/shard_map/ppermute | solution.py:31
  22.7 6.3 %collective-permute-start.9 = (bf16[2,128,256]{2,1,0:T(8,128)(2,1)S(1)}, bf16[2,128,256]{2,1,0:T(8,128)(2,1)S(1)}, u32[]{:S(2)}, u32[]{:S(2)}) collective-permute-start(bf16[2,128,256]{2,1,0:T(8,128)(2,1)S(1)} %add_convert_fusion.2), channel_id=1, source_target_pairs={{0,24},{1,25},{2,26},{3,27},{4,28},{5,29},{6,30},{7,31},{8,16},{9,... | collective-permute-start | bytes 393224 | tf_op jit(solution)/shard_map/ppermute | solution.py:31
  25.1 6.6 %collective-permute-start.11 = (bf16[2,128,256]{2,1,0:T(8,128)(2,1)S(1)}, bf16[2,128,256]{2,1,0:T(8,128)(2,1)S(1)}, u32[]{:S(2)}, u32[]{:S(2)}) collective-permute-start(bf16[2,128,256]{2,1,0:T(8,128)(2,1)S(1)} %add_convert_fusion.1), channel_id=1, source_target_pairs={{0,16},{1,17},{2,18},{3,19},{4,20},{5,21},{6,22},{7,23},{8,24},{9,... | collective-permute-start | bytes 393224 | tf_op jit(solution)/shard_map/ppermute | solution.py:31
  25.8 5.9 %collective-permute-start.13 = (bf16[2,128,256]{2,1,0:T(8,128)(2,1)S(1)}, bf16[2,128,256]{2,1,0:T(8,128)(2,1)S(1)}, u32[]{:S(2)}, u32[]{:S(2)}) collective-permute-start(bf16[2,128,256]{2,1,0:T(8,128)(2,1)S(1)} %add_convert_fusion), channel_id=1, source_target_pairs={{0,8},{1,9},{2,10},{3,11},{4,12},{5,13},{6,14},{7,15},{8,0},{9,1},... | collective-permute-start | bytes 393224 | tf_op jit(solution)/shard_map/ppermute | solution.py:31
